TPU v7x, 512 devices: a whole 4x8x8 slice. The times are simulated.
512 devices in a mesh: seq: 16 (over y, core), head: 32 (over z, x).
Axes of the slice: x: 4, y: 8, z: 8, core: 2. Of those that a mesh axis runs over, the one named last changes fastest.
Arguments:
- queries: bfloat16 [65536, 8192], P(('seq', 'head')), may hold values from -36 to 36
- keys_values: bfloat16 [65536, 2048], P(('seq', 'head')), may hold values from -14 to 14
- vertical: int32 [64, 4], replicated, may hold values from -1 to 63, as said below
- slash: int32 [64, 2], replicated, may hold values from -1 to 2, as said below
- assignment: int32 [64], replicated, may hold values from 0 to 63, as said below
Outputs:
- attended: bfloat16 [1024, 4096, 128], P(('seq', 'head'))
Inputs may be any that keep to these rules, and one draw needn't show every extreme that they name: `vertical`: row h lists distinct blocks below 64, used entries first and -1 after them; a row uses 1 to 4 entries. The rows of the 8 query heads of one key-value head name exactly 8 distinct blocks together. `slash`: row h lists distinct offsets, used entries first and -1 after them; a row uses 1 to 2 entries. `assignment`: every unit appears once. Slots 2 * d to 2 * d + 1 of a group belong to index d of the head axis, and their units are parts of query heads of one key-value head.
All inputs are finite; a program needn't handle non-finite values.
Results may differ from a plain program's by a relative error of at most 0.0065.
Values may be sent and summed in bfloat16 or wider, within the bound.
A program may use at most 64 MiB of HBM per device.

v0:
```python
import math

import jax
import jax.numpy as jnp
from jax import lax
from jax.sharding import PartitionSpec as P

HQ = 64
HK = 8
HD = 128
BLK = 64
REACH = 2
NV = 4
GQ = 8


def from_behind(value, axis, steps):
    count = lax.axis_size(axis)
    leading, last = (max(0, -steps), min(count, count - steps))
    return lax.ppermute(value, axis, [(source, source + steps) for source in range(leading, last)])


def broadcast(block, axis, holder):
    block = jnp.where(lax.axis_index(axis) == holder, block, jnp.zeros_like(block))
    return lax.psum(block, axis)


def softmax_update(state, scores, mask, product):
    top, total, accum = state
    masked = jnp.where(mask, scores, -jnp.inf)
    new_top = jnp.maximum(top, jnp.max(masked, axis=-1))
    factor = jnp.exp(top - new_top)
    weights = jnp.where(mask, jnp.exp(scores - new_top[..., None]), 0.0)
    total = total * factor + jnp.sum(weights, axis=-1)
    accum = accum * factor[..., None] + product(weights.astype(jnp.bfloat16))
    return (new_top, total, accum)


def attend_blocks(
    query_blocks,
    query_index,
    key_store,
    store_base,
    store_heads,
    vertical_store,
    vertical_slot,
    head_ids,
    vertical,
    slash,
):
    items, count, width, depth = query_blocks.shape
    scale = 1.0 / math.sqrt(depth)
    vert_rows = vertical[head_ids]
    slash_rows = slash[head_ids]
    main_steps = 1 + jnp.max(jnp.sum((slash_rows >= 1).astype(jnp.int32), axis=1))
    vertical_steps = jnp.max(jnp.sum((vert_rows >= 0).astype(jnp.int32), axis=1))
    stored = key_store.shape[0]
    causal = jnp.arange(width)[None, :] <= jnp.arange(width)[:, None]
    begin = (
        jnp.full((items, count, width), -jnp.inf, jnp.float32),
        jnp.zeros((items, count, width), jnp.float32),
        jnp.zeros((items, count, width, depth), jnp.float32),
    )

    def main_step(number, state):
        offset = jnp.where(number == 0, 0, jnp.take(slash_rows, jnp.maximum(number - 1, 0), axis=1))
        target = query_index - offset[:, None]
        repeated = jnp.any(target[:, :, None] == vert_rows[:, None, :], axis=-1)
        valid = (number == 0) | (offset[:, None] >= 1) & (target >= 0) & jnp.logical_not(repeated)
        local = jnp.clip(target - store_base, 0, stored - 1)
        fetched = key_store[local, :, store_heads[:, None]]
        keys = fetched[..., :depth]
        values = fetched[..., depth:]
        scores = (
            jnp.einsum("inqd,inkd->inqk", query_blocks, keys, preferred_element_type=jnp.float32)
            * scale
        )
        mask = valid[:, :, None, None] & ((number > 0) | causal)[None, None]
        return softmax_update(
            state,
            scores,
            mask,
            lambda weights: jnp.einsum(
                "inqk,inkd->inqd", weights, values, preferred_element_type=jnp.float32
            ),
        )

    def vertical_step(number, state):
        blocks = jnp.take(vert_rows, number, axis=1)
        valid = (blocks[:, None] >= 0) & (blocks[:, None] < query_index)
        fetched = vertical_store[jnp.take(vertical_slot, number, axis=1)]
        keys = fetched[..., :depth]
        values = fetched[..., depth:]
        scores = (
            jnp.einsum("inqd,ikd->inqk", query_blocks, keys, preferred_element_type=jnp.float32)
            * scale
        )
        mask = jnp.broadcast_to(valid[:, :, None, None], scores.shape)
        return softmax_update(
            state,
            scores,
            mask,
            lambda weights: jnp.einsum(
                "inqk,ikd->inqd", weights, values, preferred_element_type=jnp.float32
            ),
        )

    state = lax.fori_loop(0, main_steps, main_step, begin)
    state = lax.fori_loop(0, vertical_steps, vertical_step, state)
    top, total, accum = state
    return (accum / total[..., None]).astype(jnp.bfloat16)


def on_device(queries, keys_values, vertical, slash, assignment):
    rows = queries.shape[0]
    members = lax.axis_size("head")
    seq_place = lax.axis_index("seq")
    head_place = lax.axis_index("head")
    parts = max(1, 2 * members // HQ)
    per_device = parts * HQ // members
    portion = rows // parts
    device_blocks = rows // BLK
    group_blocks = device_blocks * members
    slot_major = assignment.reshape(members, per_device).T.reshape(-1)
    unit_heads = slot_major % HQ
    unit_parts = slot_major // HQ
    mine = lax.dynamic_slice_in_dim(assignment, per_device * head_place, per_device)
    my_heads = mine % HQ
    my_parts = mine // HQ
    split_queries = queries.reshape(parts, portion, HQ, HD)
    outgoing = split_queries[unit_parts, :, unit_heads].reshape(per_device, members, portion, HD)
    incoming = lax.all_to_all(outgoing, "head", split_axis=1, concat_axis=1, tiled=True)
    wanted = assignment.reshape(members, per_device)[:, 0] % HQ // GQ
    shipped = keys_values.reshape(rows, HK, 2 * HD)[:, wanted]
    group_pairs = lax.all_to_all(shipped, "head", split_axis=1, concat_axis=0, tiled=True)
    own_pairs = group_pairs[:, 0]
    group_tail = own_pairs[own_pairs.shape[0] - REACH * BLK :]
    before = from_behind(group_tail, "seq", 1)
    store_flat = jnp.concatenate([before, own_pairs], axis=0).reshape(
        REACH + group_blocks, BLK, 2 * HD
    )
    picked = store_flat[jnp.clip(vertical[my_heads], 0, None) + REACH]
    shared = broadcast(picked, "seq", 0)
    vertical_store = shared.reshape(per_device * NV, BLK, 2 * HD)
    per_portion = portion // BLK
    order = jnp.arange(members * per_portion, dtype=jnp.int32)
    query_index = (
        seq_place * group_blocks
        + (order // per_portion)[None, :] * device_blocks
        + my_parts[:, None] * per_portion
        + (order % per_portion)[None, :]
    )
    query_blocks = incoming.reshape(per_device, members * per_portion, BLK, HD)
    slot_rows = (
        jnp.arange(per_device, dtype=jnp.int32)[:, None] * NV
        + jnp.arange(NV, dtype=jnp.int32)[None, :]
    )
    outputs = attend_blocks(
        query_blocks,
        query_index,
        store_flat[:, :, None, :],
        seq_place * group_blocks - REACH,
        jnp.zeros((per_device,), jnp.int32),
        vertical_store,
        slot_rows,
        my_heads,
        vertical,
        slash,
    )
    attended = outputs.reshape(per_device, members * portion, HD)
    return attended


def solution(mesh):
    placed = (P(("seq", "head"), None), P(("seq", "head"), None), P(), P(), P())
    return jax.shard_map(
        on_device,
        mesh=mesh,
        in_specs=placed,
        out_specs=P(("seq", "head"), None, None),
        check_vma=False,
    )
```

profile of v0, /device:TPU:1, one launch (start us, length us, event | category | flops | bytes accessed | tf_op | source)
XLA Modules:
  0.0 312.2 jit_solution(15812212171097348099)
XLA Ops:
  6.5 0.7 reshape.378
  7.3 0.1 fusion.41
  7.4 1.3 copy.66
  8.8 0.2 copy.67
  9.0 2.0 gather_fusion.4
  11.0 13.7 %all-to-all-start = ((bf16[128,32,256]{2,0,1:T(8,128)(2,1)}), bf16[128,32,256]{2,0,1:T(8,128)(2,1)S(1)}, u32[]{:S(2)}, u32[]{:S(2)}) async-start(bf16[128,32,256]{2,0,1:T(8,128)(2,1)} %bitcast.108), calls=%async_computation | async-start | bytes 4194304 | tf_op jit(solution)/shard_map/all_to_all | solution.py:135
  24.9 4.1 %copy.68 = bf16[128,8192]{0,1:T(8,128)(2,1)} copy(bf16[128,8192]{1,0:T(8,128)(2,1)} %param.11) | data formatting | bytes 4194304 | tf_op args[0]
  28.9 4.1 %copy.70 = bf16[1,128,64,128]{3,1,2,0:T(8,128)(2,1)} copy(bf16[1,128,64,128]{1,3,2,0:T(8,128)(2,1)} %bitcast.110) | data formatting | bytes 4194304 | tf_op jit(solution)/shard_map/reshape | solution.py:130
  33.1 3.7 %gather_fusion.5 = bf16[64,128,128]{2,1,0:T(8,128)(2,1)} fusion(bf16[1,128,64,128]{3,1,2,0:T(8,128)(2,1)} %copy.70, s32[64]{0:T(128)S(1)} %fusion.52), kind=kCustom, calls=%fused_computation.5 | custom fusion | bytes 4194816 | tf_op jit(solution)/shard_map/gather | solution.py:131
  36.8 3.2 %copy.71 = bf16[2,32,128,128]{3,2,0,1:T(8,128)(2,1)} copy(bf16[2,32,128,128]{3,2,1,0:T(8,128)(2,1)} %bitcast.109) | data formatting | bytes 4194304 | tf_op jit(solution)/shard_map/reshape | solution.py:131
  40.0 33.2 %all-to-all-done = bf16[128,32,256]{2,0,1:T(8,128)(2,1)S(1)} async-done(((bf16[128,32,256]{2,0,1:T(8,128)(2,1)}), bf16[128,32,256]{2,0,1:T(8,128)(2,1)S(1)}, u32[]{:S(2)}, u32[]{:S(2)}) %all-to-all-start) | async-done | bytes 2097184 | tf_op jit(solution)/shard_map/all_to_all | solution.py:135
  73.2 6.7 %all-to-all-start.1 = ((bf16[2,32,128,128]{3,2,0,1:T(8,128)(2,1)}), bf16[2,32,128,128]{3,2,0,1:T(8,128)(2,1)}, u32[]{:S(2)}, u32[]{:S(2)}) async-start(bf16[2,32,128,128]{3,2,0,1:T(8,128)(2,1)} %copy.71), calls=%async_computation.1 | async-start | bytes 4194304 | tf_op jit(solution)/shard_map/all_to_all | solution.py:132
  80.0 0.1 copy.65
  80.1 0.1 copy.64
  80.3 0.6 gather_fusion.3
  80.9 0.6 gather_fusion.2
  81.4 0.1 copy.73
  81.5 0.1 copy.75
  81.7 0.1 fusion.43
  81.8 0.6 reduce_max.39
  82.5 0.1 fusion.44
  82.6 0.7 reduce_max.40
  83.8 5.1 %collective-permute-start = (bf16[128,256]{1,0:T(8,128)(2,1)S(1)}, bf16[128,256]{1,0:T(8,128)(2,1)S(1)}, u32[]{:S(2)}, u32[]{:S(2)}) collective-permute-start(bf16[128,256]{1,0:T(8,128)(2,1)S(1)} %slice_bitcast_fusion.4), channel_id=1, source_target_pairs={{0,32},{32,64},{64,96},{96,128},{128,160},{160,192},{192,224},{224... | collective-permute-start | bytes 196616 | tf_op jit(solution)/shard_map/ppermute | solution.py:20
  88.9 38.2 %all-to-all-done.1 = bf16[2,32,128,128]{3,2,0,1:T(8,128)(2,1)} async-done(((bf16[2,32,128,128]{3,2,0,1:T(8,128)(2,1)}), bf16[2,32,128,128]{3,2,0,1:T(8,128)(2,1)}, u32[]{:S(2)}, u32[]{:S(2)}) %all-to-all-start.1) | async-done | bytes 2097184 | tf_op jit(solution)/shard_map/all_to_all | solution.py:132
  127.1 3.2 %copy.72 = bf16[2,32,128,128]{3,2,1,0:T(8,128)(2,1)} copy(bf16[2,32,128,128]{3,2,0,1:T(8,128)(2,1)} %all-to-all-done.1) | data formatting | bytes 4194304 | tf_op jit(solution)/shard_map/all_to_all | solution.py:132
  130.3 1.7 pad_maximum_fusion
  132.1 0.6 gather_fusion.6
  132.6 0.7 broadcast_select_fusion.4
  133.4 2.5 broadcast_in_dim.93
  135.9 45.2 %while.34 = (s32[]{:T(128)}, f32[2,64,64]{2,1,0:T(8,128)S(1)}, f32[2,64,64]{2,1,0:T(8,128)S(1)}, f32[2,64,64,128]{3,2,1,0:T(8,128)}, s32[]{:T(128)}, /*index=5*/...) while((s32[]{:T(128)}, f32[2,64,64]{2,1,0:T(8,128)S(1)}, ...), condition=%wide.region_6.7_spmd.clone, body=%wide.region_2.6_spmd.clone.sunk | while | flops 277900800 | bytes 48851412 | solution.py:108
  136.3 2.8 gather_fusion
  139.1 3.5 %fusion.73 = (f32[2,64,64]{2,1,0:T(8,128)S(1)}, f32[2,64,64,64]{3,2,1,0:T(8,128)S(1)}) fusion(pred[64,64]{0,1:T(8,128)(4,1)S(1)} %fusion.70, pred[2,64]{1,0:T(4,128)(4,1)S(1)} %and_or_fusion.2, bf16[2,64,64,128]{3,2,1,0:T(8,128)(2,1)} %get-tuple-element.741, bf16[2,64,64,256]{3,2,1,0:T(8,128)(2,1)} %bitcast.103), kind=kOutput, calls=%fused_computation.13.clone.1 | convolution fusion | flops 136306688 | bytes 6328448 | tf_op jit(solution)/shard_map/while/body/inqd,inkd->inqk/dot_general | solution.py:75
  142.6 1.4 fusion.74
  144.0 0.8 copy-done
  144.8 6.1 %multiply_add_fusion.9 = f32[2,64,64,128]{3,2,1,0:T(8,128)} fusion(f32[2,64,64,128]{3,2,1,0:T(8,128)} %get-tuple-element.719, f32[2,64,64,64]{3,2,1,0:T(8,128)S(1)} %get-tuple-element.679, bf16[2,64,64,256]{3,2,1,0:T(8,128)(2,1)S(1)} %bitcast.104, f32[2,64,64]{2,1,0:T(8,128)S(1)} %get-tuple-element.681, f32[2,64,64]{2,1,0:T(8,128)S(1)} %max.42, ...), kind=kOutput, calls=%fused_computation.16.clone.1 | convolution fusion | flops 138936320 | bytes 14819840 | tf_op jit(solution)/shard_map/while/body/inqk,inkd->inqd/dot_general | solution.py:83
  151.4 2.8 gather_fusion
  154.2 3.5 %fusion.73 = (f32[2,64,64]{2,1,0:T(8,128)S(1)}, f32[2,64,64,64]{3,2,1,0:T(8,128)S(1)}) fusion(pred[64,64]{0,1:T(8,128)(4,1)S(1)} %fusion.70, pred[2,64]{1,0:T(4,128)(4,1)S(1)} %and_or_fusion.2, bf16[2,64,64,128]{3,2,1,0:T(8,128)(2,1)} %get-tuple-element.741, bf16[2,64,64,256]{3,2,1,0:T(8,128)(2,1)} %bitcast.103), kind=kOutput, calls=%fused_computation.13.clone.1 | convolution fusion | flops 136306688 | bytes 6328448 | tf_op jit(solution)/shard_map/while/body/inqd,inkd->inqk/dot_general | solution.py:75
  157.7 1.4 fusion.74
  159.1 0.8 copy-done
  159.9 6.1 %multiply_add_fusion.9 = f32[2,64,64,128]{3,2,1,0:T(8,128)} fusion(f32[2,64,64,128]{3,2,1,0:T(8,128)} %get-tuple-element.719, f32[2,64,64,64]{3,2,1,0:T(8,128)S(1)} %get-tuple-element.679, bf16[2,64,64,256]{3,2,1,0:T(8,128)(2,1)S(1)} %bitcast.104, f32[2,64,64]{2,1,0:T(8,128)S(1)} %get-tuple-element.681, f32[2,64,64]{2,1,0:T(8,128)S(1)} %max.42, ...), kind=kOutput, calls=%fused_computation.16.clone.1 | convolution fusion | flops 138936320 | bytes 14819840 | tf_op jit(solution)/shard_map/while/body/inqk,inkd->inqd/dot_general | solution.py:83
  166.4 2.8 gather_fusion
  169.2 3.5 %fusion.73 = (f32[2,64,64]{2,1,0:T(8,128)S(1)}, f32[2,64,64,64]{3,2,1,0:T(8,128)S(1)}) fusion(pred[64,64]{0,1:T(8,128)(4,1)S(1)} %fusion.70, pred[2,64]{1,0:T(4,128)(4,1)S(1)} %and_or_fusion.2, bf16[2,64,64,128]{3,2,1,0:T(8,128)(2,1)} %get-tuple-element.741, bf16[2,64,64,256]{3,2,1,0:T(8,128)(2,1)} %bitcast.103), kind=kOutput, calls=%fused_computation.13.clone.1 | convolution fusion | flops 136306688 | bytes 6328448 | tf_op jit(solution)/shard_map/while/body/inqd,inkd->inqk/dot_general | solution.py:75
  172.7 1.4 fusion.74
  174.1 0.8 copy-done
  174.9 6.1 %multiply_add_fusion.9 = f32[2,64,64,128]{3,2,1,0:T(8,128)} fusion(f32[2,64,64,128]{3,2,1,0:T(8,128)} %get-tuple-element.719, f32[2,64,64,64]{3,2,1,0:T(8,128)S(1)} %get-tuple-element.679, bf16[2,64,64,256]{3,2,1,0:T(8,128)(2,1)S(1)} %bitcast.104, f32[2,64,64]{2,1,0:T(8,128)S(1)} %get-tuple-element.681, f32[2,64,64]{2,1,0:T(8,128)S(1)} %max.42, ...), kind=kOutput, calls=%fused_computation.16.clone.1 | convolution fusion | flops 138936320 | bytes 14819840 | tf_op jit(solution)/shard_map/while/body/inqk,inkd->inqd/dot_general | solution.py:83
  181.1 66.8 %all-reduce.3.cloned.1.call-done = bf16[8,64,256]{2,1,0:T(8,128)(2,1)} async-done(((bf16[8,64,256]{2,1,0:T(8,128)(2,1)}), bf16[8,64,256]{2,1,0:T(8,128)(2,1)}) %all-reduce.3.cloned.1.call-update) | async-done | bytes 262160 | tf_op jit(solution)/shard_map/psum | solution.py:25
  247.9 53.7 %while.35 = (s32[]{:T(128)}, f32[2,64,64]{2,1,0:T(8,128)S(1)}, f32[2,64,64]{2,1,0:T(8,128)S(1)}, f32[2,64,64,128]{3,2,1,0:T(8,128)}, s32[]{:T(128)}, /*index=5*/...) while((s32[]{:T(128)}, f32[2,64,64]{2,1,0:T(8,128)S(1)}, ...), condition=%wide.region_13.15_spmd.clone, body=%wide.region_10.14_spmd.clone.sunk | while | flops 276317728 | bytes 19667008 | solution.py:109
  248.6 1.5 gather_fusion.1
  250.1 3.7 %select_reduce_fusion.2 = (f32[2,64,64]{2,1,0:T(8,128)S(1)}, f32[2,64,64,64]{3,1,2,0:T(8,128)S(1)}) fusion(pred[2,64]{1,0:T(4,128)(4,1)S(1)} %compare_and_fusion.2, bf16[2,64,64,128]{3,2,1,0:T(8,128)(2,1)} %get-tuple-element.787, bf16[2,64,256]{2,1,0:T(8,128)(2,1)S(1)} %gather_fusion.1), kind=kOutput, calls=%fused_computation.51.clone.1 | convolution fusion | flops 135782400 | bytes 4260352 | tf_op jit(solution)/shard_map/while/body/inqd,ikd->inqk/dot_general | solution.py:95
  253.9 1.1 bitcast_reduce_fusion.2
  255.0 6.1 %multiply_add_fusion.11 = f32[2,64,64,128]{3,2,1,0:T(8,128)} fusion(f32[2,64,64,128]{3,2,1,0:T(8,128)} %get-tuple-element.767, f32[2,64,64,64]{3,1,2,0:T(8,128)S(1)} %get-tuple-element.697, f32[2,64,64]{2,1,0:T(8,128)S(1)} %get-tuple-element.699, f32[2,64,64]{2,1,0:T(8,128)S(1)} %max.43, pred[2,64]{1,0:T(4,128)(4,1)S(1)} %compare_and_fusion.2, ...), kind=kOutput, calls=%fused_computation.49.clone.1 | convolution fusion | flops 138412032 | bytes 12747264 | tf_op jit(solution)/shard_map/while/body/inqk,ikd->inqd/dot_general | solution.py:103
  261.9 1.5 gather_fusion.1
  263.4 3.7 %select_reduce_fusion.2 = (f32[2,64,64]{2,1,0:T(8,128)S(1)}, f32[2,64,64,64]{3,1,2,0:T(8,128)S(1)}) fusion(pred[2,64]{1,0:T(4,128)(4,1)S(1)} %compare_and_fusion.2, bf16[2,64,64,128]{3,2,1,0:T(8,128)(2,1)} %get-tuple-element.787, bf16[2,64,256]{2,1,0:T(8,128)(2,1)S(1)} %gather_fusion.1), kind=kOutput, calls=%fused_computation.51.clone.1 | convolution fusion | flops 135782400 | bytes 4260352 | tf_op jit(solution)/shard_map/while/body/inqd,ikd->inqk/dot_general | solution.py:95
  267.2 1.1 bitcast_reduce_fusion.2
  268.3 6.1 %multiply_add_fusion.11 = f32[2,64,64,128]{3,2,1,0:T(8,128)} fusion(f32[2,64,64,128]{3,2,1,0:T(8,128)} %get-tuple-element.767, f32[2,64,64,64]{3,1,2,0:T(8,128)S(1)} %get-tuple-element.697, f32[2,64,64]{2,1,0:T(8,128)S(1)} %get-tuple-element.699, f32[2,64,64]{2,1,0:T(8,128)S(1)} %max.43, pred[2,64]{1,0:T(4,128)(4,1)S(1)} %compare_and_fusion.2, ...), kind=kOutput, calls=%fused_computation.49.clone.1 | convolution fusion | flops 138412032 | bytes 12747264 | tf_op jit(solution)/shard_map/while/body/inqk,ikd->inqd/dot_general | solution.py:103
  275.1 1.5 gather_fusion.1
  276.7 3.7 %select_reduce_fusion.2 = (f32[2,64,64]{2,1,0:T(8,128)S(1)}, f32[2,64,64,64]{3,1,2,0:T(8,128)S(1)}) fusion(pred[2,64]{1,0:T(4,128)(4,1)S(1)} %compare_and_fusion.2, bf16[2,64,64,128]{3,2,1,0:T(8,128)(2,1)} %get-tuple-element.787, bf16[2,64,256]{2,1,0:T(8,128)(2,1)S(1)} %gather_fusion.1), kind=kOutput, calls=%fused_computation.51.clone.1 | convolution fusion | flops 135782400 | bytes 4260352 | tf_op jit(solution)/shard_map/while/body/inqd,ikd->inqk/dot_general | solution.py:95
  280.4 1.1 bitcast_reduce_fusion.2
  281.6 6.1 %multiply_add_fusion.11 = f32[2,64,64,128]{3,2,1,0:T(8,128)} fusion(f32[2,64,64,128]{3,2,1,0:T(8,128)} %get-tuple-element.767, f32[2,64,64,64]{3,1,2,0:T(8,128)S(1)} %get-tuple-element.697, f32[2,64,64]{2,1,0:T(8,128)S(1)} %get-tuple-element.699, f32[2,64,64]{2,1,0:T(8,128)S(1)} %max.43, pred[2,64]{1,0:T(4,128)(4,1)S(1)} %compare_and_fusion.2, ...), kind=kOutput, calls=%fused_computation.49.clone.1 | convolution fusion | flops 138412032 | bytes 12747264 | tf_op jit(solution)/shard_map/while/body/inqk,ikd->inqd/dot_general | solution.py:103
  288.4 1.5 gather_fusion.1
  289.9 3.7 %select_reduce_fusion.2 = (f32[2,64,64]{2,1,0:T(8,128)S(1)}, f32[2,64,64,64]{3,1,2,0:T(8,128)S(1)}) fusion(pred[2,64]{1,0:T(4,128)(4,1)S(1)} %compare_and_fusion.2, bf16[2,64,64,128]{3,2,1,0:T(8,128)(2,1)} %get-tuple-element.787, bf16[2,64,256]{2,1,0:T(8,128)(2,1)S(1)} %gather_fusion.1), kind=kOutput, calls=%fused_computation.51.clone.1 | convolution fusion | flops 135782400 | bytes 4260352 | tf_op jit(solution)/shard_map/while/body/inqd,ikd->inqk/dot_general | solution.py:95
  293.7 1.1 bitcast_reduce_fusion.2
  294.8 6.1 %multiply_add_fusion.11 = f32[2,64,64,128]{3,2,1,0:T(8,128)} fusion(f32[2,64,64,128]{3,2,1,0:T(8,128)} %get-tuple-element.767, f32[2,64,64,64]{3,1,2,0:T(8,128)S(1)} %get-tuple-element.697, f32[2,64,64]{2,1,0:T(8,128)S(1)} %get-tuple-element.699, f32[2,64,64]{2,1,0:T(8,128)S(1)} %max.43, pred[2,64]{1,0:T(4,128)(4,1)S(1)} %compare_and_fusion.2, ...), kind=kOutput, calls=%fused_computation.49.clone.1 | convolution fusion | flops 138412032 | bytes 12747264 | tf_op jit(solution)/shard_map/while/body/inqk,ikd->inqd/dot_general | solution.py:103
  301.5 3.8 %divide_convert_fusion = bf16[2,64,64,128]{3,2,1,0:T(8,128)(2,1)} fusion(f32[2,64,64,128]{3,2,1,0:T(8,128)} %get-tuple-element.217, f32[2,64,64]{2,1,0:T(8,128)S(1)} %get-tuple-element.218), kind=kLoop, calls=%fused_computation.72 | loop fusion | flops 2097152 | bytes 6324224 | tf_op jit(solution)/shard_map/convert_element_type | solution.py:111
  (91 shorter events, 2.6 us)
Async XLA Ops:
  11.0 62.2 %all-to-all-start = ((bf16[128,32,256]{2,0,1:T(8,128)(2,1)}), bf16[128,32,256]{2,0,1:T(8,128)(2,1)S(1)}, u32[]{:S(2)}, u32[]{:S(2)}) async-start(bf16[128,32,256]{2,0,1:T(8,128)(2,1)} %bitcast.108), calls=%async_computation | async-start | bytes 4194304 | tf_op jit(solution)/shard_map/all_to_all | solution.py:135
  36.8 43.2 %copy-start.2 = (s32[64,4]{0,1:T(4,128)S(1)}, s32[64,4]{0,1:T(4,128)}, u32[]{:S(2)}) copy-start(s32[64,4]{0,1:T(4,128)} %param.13) | copy-start | bytes 3076
  36.8 43.3 %copy-start.4 = (s32[64,2]{0,1:T(2,128)S(1)}, s32[64,2]{0,1:T(2,128)}, u32[]{:S(2)}) copy-start(s32[64,2]{0,1:T(2,128)} %param.14) | copy-start | bytes 1540
  36.8 43.4 %copy-start.3 = (s32[64]{0:T(128)S(1)}, s32[64]{0:T(128)}, u32[]{:S(2)}) copy-start(s32[64]{0:T(128)} %param.15) | copy-start | bytes 772
  73.2 57.2 %copy-start.1 = (bf16[128,32,256]{2,0,1:T(8,128)(2,1)}, bf16[128,32,256]{2,0,1:T(8,128)(2,1)S(1)}, u32[]{:S(2)}) copy-start(bf16[128,32,256]{2,0,1:T(8,128)(2,1)S(1)} %all-to-all-done) | copy-start | bytes 6291460
  73.2 53.9 %all-to-all-start.1 = ((bf16[2,32,128,128]{3,2,0,1:T(8,128)(2,1)}), bf16[2,32,128,128]{3,2,0,1:T(8,128)(2,1)}, u32[]{:S(2)}, u32[]{:S(2)}) async-start(bf16[2,32,128,128]{3,2,0,1:T(8,128)(2,1)} %copy.71), calls=%async_computation.1 | async-start | bytes 4194304 | tf_op jit(solution)/shard_map/all_to_all | solution.py:132
  79.9 167.9 %all-reduce.3.cloned.1.call-start = ((), (), s32[]{:S(2)}) async-start(), calls=%async_computation.2 | async-start | bytes 524288 | tf_op jit(solution)/shard_map/psum | solution.py:25
  83.8 46.5 %collective-permute-start = (bf16[128,256]{1,0:T(8,128)(2,1)S(1)}, bf16[128,256]{1,0:T(8,128)(2,1)S(1)}, u32[]{:S(2)}, u32[]{:S(2)}) collective-permute-start(bf16[128,256]{1,0:T(8,128)(2,1)S(1)} %slice_bitcast_fusion.4), channel_id=1, source_target_pairs={{0,32},{32,64},{64,96},{96,128},{128,160},{160,192},{192,224},{224... | collective-permute-start | bytes 196616 | tf_op jit(solution)/shard_map/ppermute | solution.py:20
  142.6 2.2 copy-start
  157.6 2.2 copy-start
  172.7 2.2 copy-start
Sparse Core Ops, SparseCore 0:
  133.5 114.2 all-reduce.2
where the time goes:
time: 314 us; the launch traced here: 312 us
  waiting for transfers between devices  138 us (44%)
  matrix products  68 us (22%)
  local copies, waits for them, and re-layouts  44.4 us (14%)
  starting transfers between devices  25.6 us (8%)
  other arithmetic  18.4 us (6%)
  between operations  14.1 us (4%)
  loops' own time  3.51 us (1%)
    psum x1, waiting for transfers between devices, broadcast(): return lax.psum(block, axis)  66.8 us
    all_to_all x1, waiting for transfers between devices, on_device(): lax.all_to_all(outgoing, 'head', split_axis=1, concat_axis=1, tiled=True)  38.2 us
    all_to_all x1, waiting for transfers between devices, on_device(): lax.all_to_all(shipped, 'head', split_axis=1, concat_axis=0, tiled=True)  33.2 us
    dot_general x4, matrix products, vertical_step(): jnp.einsum('inqk,ikd->inqd', weights, values, preferred_element_type=jnp....  24.2 us
    dot_general x3, matrix products, main_step(): jnp.einsum('inqk,inkd->inqd', weights, values, preferred_element_type=jnp...  18.4 us
    dot_general x4, matrix products, vertical_step(): jnp.einsum('inqd,ikd->inqk', query_blocks, keys, preferred_element_type=j...  14.9 us
    all_to_all x1, starting transfers between devices, on_device(): lax.all_to_all(shipped, 'head', split_axis=1, concat_axis=0, tiled=True)  13.7 us
    dot_general x3, matrix products, main_step(): jnp.einsum('inqd,inkd->inqk', query_blocks, keys, preferred_element_type=...  10.4 us
  transfers between devices with their start and end apart: 4, of which 3 were waited for; matrix products, arithmetic and copies ran while one was open for 21% of the time, Pallas kernels for 0%

commit v1 on v0

v1 whole, which is shorter than its diff:
```python
import functools
import math

import jax
import jax.numpy as jnp
from jax import lax
from jax.experimental import pallas as pl
from jax.experimental.pallas import tpu as pltpu
from jax.sharding import PartitionSpec as P

HD = 128
BLK = 64
NV = 4
NX = 4
CH = 16
NC = BLK // CH
ROWS = 2 * BLK
VPOOL = 8
HIDE = -1e30
MESH = pl.DeviceIdType.MESH


def table_kernel(group, vert_ref, assign_ref, out_ref):
    v = vert_ref[...]
    heads = v.shape[0]
    block = lax.broadcasted_iota(jnp.int32, (heads, BLK), 1)
    used = jnp.zeros((heads, BLK), jnp.float32)
    for n in range(NV):
        used = jnp.maximum(used, (v[:, n : n + 1] == block).astype(jnp.float32))
    one = lax.broadcasted_iota(jnp.int32, (heads, heads), 0)
    other = lax.broadcasted_iota(jnp.int32, (heads, heads), 1)
    same = (one // group == other // group).astype(jnp.float32)
    some = jnp.dot(same, used, preferred_element_type=jnp.float32)
    pool = (some > 0.5).astype(jnp.float32)
    before = (
        lax.broadcasted_iota(jnp.int32, (BLK, BLK), 0)
        < lax.broadcasted_iota(jnp.int32, (BLK, BLK), 1)
    ).astype(jnp.float32)
    rank = jnp.dot(pool, before, preferred_element_type=jnp.float32)
    lane = lax.broadcasted_iota(jnp.int32, (heads, HD), 1)
    table = jnp.zeros((heads, HD), jnp.float32)
    for n in range(NV):
        place = jnp.sum(jnp.where(v[:, n : n + 1] == block, rank, 0.0), axis=1, keepdims=True)
        table = jnp.where(lane == n, place, table)
    number = block.astype(jnp.float32)
    for r in range(VPOOL):
        held = (pool > 0.5) & (rank > r - 0.5) & (rank < r + 0.5)
        place = jnp.sum(jnp.where(held, number, 0.0), axis=1, keepdims=True)
        table = jnp.where(lane == 8 + r, place, table)
    head = lax.broadcasted_iota(jnp.int32, (heads, HD), 0)
    table = jnp.where(lane == 4, head.astype(jnp.float32), table)
    table = jnp.where(lane == 5, (head // group).astype(jnp.float32), table)
    chosen = (assign_ref[...] % heads == other).astype(jnp.float32)
    out_ref[:heads] = table.astype(jnp.int32)
    slots = jnp.dot(chosen, table, preferred_element_type=jnp.float32)
    out_ref[heads:] = slots.astype(jnp.int32)


def main_kernel(
    sizes,
    table,
    vert_ref,
    slash_ref,
    q_hbm,
    kv_hbm,
    out,
    q_v,
    kcat,
    tbuf,
    piece,
    pool,
    stage,
    rows_bias,
    causal_bias,
    sems,
    bar_free,
):
    NS, NH, NZ, NY, HQ, HK = sizes
    GQ = HQ // HK
    owners = 2 * HK * NC
    seq = lax.axis_index("seq")
    head = lax.axis_index("head")
    y, core = seq // 2, seq % 2
    z, x = head // NX, head % NX
    a = y + core * (z - y)
    b = z + core * (y - z)

    def device(core_, a_, b_, x_):
        y_ = a_ + core_ * (b_ - a_)
        z_ = b_ + core_ * (a_ - b_)
        return y_ * 2 + core_, z_ * NX + x_

    def home(a_, c_):
        return (a_ + 2 * c_) % NZ

    owner = b == home(a, x)
    source = seq == 0
    one = jnp.int32(1)
    nil = jnp.int32(0)
    own_source = jnp.where(owner & source, one, nil)

    def columns(n):
        return pl.ds(pl.multiple_of(n * HD, HD), HD)

    @pl.loop(0, HQ)
    def _(n):
        pltpu.make_async_copy(q_hbm.at[:, columns(n)], q_v.at[n], sems.at[0]).start()

    @pl.loop(0, 2 * HK)
    def _(n):
        pltpu.make_async_copy(kv_hbm.at[:, :, :, columns(n)], kcat.at[n, 1], sems.at[1]).start()

    barrier = pltpu.get_barrier_semaphore()

    def greet(s_, h_):
        pl.semaphore_signal(barrier, inc=1, device_id=(s_, h_), device_id_type=MESH)

    @pl.when(owner)
    def _():
        @pl.loop(0, NH)
        def _(s):
            @pl.when(jnp.logical_not(source & (head == s)))
            def _():
                greet(0, s)

    @pl.loop(1, NH)
    def _(k):
        greet(seq, (head + k) % NH)

    @pl.loop(1, NY)
    def _(k):
        other = (y + k) % NY * 2 + core
        greet(other, head)

        @pl.when(core == 1)
        def _():
            for dx in range(1, NX):
                greet(other, z * NX + (x + dx) % NX)

    greet(y * 2 + 1 - core, head)

    @pl.when((head == 0) & (seq > 0))
    def _():
        greet(seq - 1, NH - 1)

    base = (seq * NH + head) * 2
    vert = vert_ref[...]
    slash = slash_ref[...]
    lane = lax.broadcasted_iota(jnp.int32, (HQ, 8 * BLK), 1) // BLK
    target = base + lane - 2
    listed = jnp.full((HQ, 8 * BLK), -1, jnp.int32)
    fresh = (target >= 0) & (lane < 4)
    for n in range(NV):
        col = vert[:, n : n + 1]
        listed = jnp.where(lane == 4 + n, col, listed)
        fresh = fresh & (target != col)
    for qb in range(2):
        off = qb + 2 - lane
        hit = (off >= 1) & ((slash[:, 0:1] == off) | (slash[:, 1:2] == off)) & fresh
        near = (lane < 4) & ((off == 0) | hit)
        far = (lane >= 4) & (listed >= 0) & (listed < base + qb)
        rows_bias[qb, :, 0] = jnp.where(near | far, 0.0, HIDE)
    row = lax.broadcasted_iota(jnp.int32, (ROWS, 2 * ROWS), 0)
    col = lax.broadcasted_iota(jnp.int32, (ROWS, 2 * ROWS), 1) - ROWS
    causal_bias[...] = jnp.where(col <= row, 0.0, HIDE)

    count = (NH - 1) + (NY - 1) * (1 + (NX - 1) * core) + 1
    count = count + jnp.where((head == NH - 1) & (seq < NS - 1), one, nil)
    count = count + jnp.where(source, owners - own_source, nil)
    pl.semaphore_wait(barrier, count)

    def remote(src, dst, send, recv, to):
        return pltpu.make_async_remote_copy(
            src_ref=src,
            dst_ref=dst,
            send_sem=sems.at[send],
            recv_sem=sems.at[recv],
            device_id=to,
            device_id_type=MESH,
        )

    def await_bytes(ref, sem):
        pltpu.make_async_copy(ref, ref, sems.at[sem]).wait()

    @pl.when(source)
    def _():
        @pl.loop(0, owners)
        def _(o):
            core_, a_, c_ = o // (HK * NC), o // NC % HK, o % NC
            s_, h_ = device(core_, a_, home(a_, c_), c_)
            src = kv_hbm.at[:, c_, :, columns(2 * a_ + core_)]
            dst = tbuf.at[pl.ds(2 * head, 2)]
            mine = (s_ == seq) & (h_ == head)

            @pl.when(mine)
            def _():
                pltpu.make_async_copy(src, dst, sems.at[3]).start()

            @pl.when(jnp.logical_not(mine))
            def _():
                remote(src, dst, 2, 3, (s_, h_)).start()

    last = (seq == NS - 1) & (head == NH - 1)
    first = (seq == 0) & (head == 0)
    wrap = jnp.where(head == NH - 1, one, nil)

    @pl.when(jnp.logical_not(last))
    def _():
        @pl.loop(0, 2 * HK)
        def _(n):
            src = kv_hbm.at[:, :, :, columns(n)]
            remote(src, kcat.at[n, 0], 4, 5, (seq + wrap, (head + 1) % NH)).start()

    @pl.when(first)
    def _():
        kcat[:, 0] = jnp.zeros((2 * HK, *kcat.shape[2:]), kcat.dtype)

    @pl.when(owner)
    def _():
        await_bytes(tbuf, 3)
        for r in range(VPOOL):
            piece[r] = tbuf[table[a * GQ, 8 + r]]

        @pl.loop(0, NZ * NX)
        def _(k):
            b_, x_ = k // NX, k % NX
            mine = (b_ == b) & (x_ == x)
            dst = pool.at[core, a, :, x]

            @pl.when(mine)
            def _():
                pltpu.make_async_copy(piece, dst, sems.at[7]).start()

            @pl.when(jnp.logical_not(mine))
            def _():
                remote(piece, dst, 6, 7, device(core, a, b_, x_)).start()

    await_bytes(pool.at[core, a], 7)

    @pl.loop(1, NY)
    def _(k):
        remote(pool.at[core, a], pool.at[core, a], 8, 9, device(core, (a + k) % NY, b, x)).start()

    await_bytes(pool.at[core, pl.ds(0, NY - 1)], 9)
    swap = remote(pool.at[core], pool.at[core], 10, 11, (y * 2 + 1 - core, head))
    swap.start()
    await_bytes(q_v, 0)
    await_bytes(kcat.at[:, 1], 1)

    @pl.when(jnp.logical_not(first))
    def _():
        await_bytes(kcat.at[:, 0], 5)

    await_bytes(pool.at[1 - core], 11)

    factor = math.log2(math.e) / math.sqrt(HD)
    contract = (((1,), (1,)), ((), ()))

    def attend(slot):
        h = table[HQ + slot, 4]
        c = table[HQ + slot, 5]
        query = q_v[h]
        keys = kcat[2 * c].reshape(2 * ROWS, HD)
        values = kcat[2 * c + 1].reshape(2 * ROWS, HD)
        places = [table[HQ + slot, n] for n in range(NV)]
        far_keys = jnp.concatenate([pool[0, c, p].reshape(BLK, HD) for p in places], axis=0)
        far_values = jnp.concatenate([pool[1, c, p].reshape(BLK, HD) for p in places], axis=0)
        bias = jnp.concatenate(
            [jnp.broadcast_to(rows_bias[qb, h], (BLK, 8 * BLK)) for qb in range(2)],
            axis=0,
        )
        near = lax.dot_general(query, keys, contract, preferred_element_type=jnp.float32)
        far = lax.dot_general(query, far_keys, contract, preferred_element_type=jnp.float32)
        near = near * factor + (bias[:, : 2 * ROWS] + causal_bias[...])
        far = far * factor + bias[:, 2 * ROWS :]
        top = jnp.maximum(
            jnp.max(near, axis=1, keepdims=True), jnp.max(far, axis=1, keepdims=True)
        )
        near = jnp.exp2(near - top)
        far = jnp.exp2(far - top)
        total = jnp.sum(near, axis=1, keepdims=True) + jnp.sum(far, axis=1, keepdims=True)
        numer = jnp.dot(
            near.astype(jnp.bfloat16), values, preferred_element_type=jnp.float32
        ) + jnp.dot(far.astype(jnp.bfloat16), far_values, preferred_element_type=jnp.float32)
        stage[slot] = (numer / total).astype(jnp.bfloat16)

    here = pl.ds(pl.multiple_of(head * ROWS, ROWS), ROWS)

    @pl.loop(1, NH + 1)
    def _(k):
        d = (head + k) % NH
        attend(2 * d)
        attend(2 * d + 1)
        src = stage.at[pl.ds(2 * d, 2)]
        dst = out.at[:, here]

        @pl.when(k == NH)
        def _():
            pltpu.make_async_copy(src, dst, sems.at[13]).start()

        @pl.when(k < NH)
        def _():
            remote(src, dst, 12, 13, (seq, d)).start()

    await_bytes(out, 13)
    await_bytes(stage.at[pl.ds(0, 2 * NH - 2)], 12)
    await_bytes(pool.at[core], 10)
    await_bytes(pool.at[core, pl.ds(0, NY - 1)], 8)

    @pl.when(owner)
    def _():
        await_bytes(stage.at[pl.ds(0, NZ * NX - 1)], 6)

    @pl.when(jnp.logical_not(last))
    def _():
        await_bytes(kv_hbm, 4)

    @pl.when(source & owner)
    def _():
        await_bytes(stage.at[pl.ds(0, owners - 1), pl.ds(0, 32)], 2)

    @pl.when(source & jnp.logical_not(owner))
    def _():
        await_bytes(stage.at[pl.ds(0, owners), pl.ds(0, 32)], 2)


def on_device(sizes, queries, keys_values, vertical, slash, assignment):
    NS, NH, NZ, NY, HQ, HK = sizes
    width = keys_values.shape[1]
    vmem = pl.BlockSpec(memory_space=pltpu.VMEM)
    smem = pl.BlockSpec(memory_space=pltpu.SMEM)
    hbm = pl.BlockSpec(memory_space=pl.ANY)
    table = pl.pallas_call(
        functools.partial(table_kernel, HQ // HK),
        out_shape=jax.ShapeDtypeStruct((2 * HQ, HD), jnp.int32),
        in_specs=[vmem, vmem],
        out_specs=vmem,
    )(vertical, assignment.reshape(HQ, 1))
    return pl.pallas_call(
        functools.partial(main_kernel, sizes),
        out_shape=jax.ShapeDtypeStruct((2, NH * ROWS, HD), jnp.bfloat16),
        in_specs=[smem, vmem, vmem, hbm, hbm],
        out_specs=hbm,
        scratch_shapes=[
            pltpu.VMEM((HQ, ROWS, HD), jnp.bfloat16),
            pltpu.VMEM((2 * HK, 2, 2, NC, CH, HD), jnp.bfloat16),
            pltpu.VMEM((2 * NH, CH, HD), jnp.bfloat16),
            pltpu.VMEM((VPOOL, CH, HD), jnp.bfloat16),
            pltpu.VMEM((2, HK, VPOOL, NC, CH, HD), jnp.bfloat16),
            pltpu.VMEM((max(2 * NH, 2 * HK * NC), ROWS, HD), jnp.bfloat16),
            pltpu.VMEM((2, HQ, 1, 8 * BLK), jnp.float32),
            pltpu.VMEM((ROWS, 2 * ROWS), jnp.float32),
            pltpu.SemaphoreType.DMA((14,)),
            pltpu.SemaphoreType.REGULAR,
        ],
        compiler_params=pltpu.CompilerParams(
            collective_id=0, has_side_effects=True, vmem_limit_bytes=40 * 2**20
        ),
    )(table, vertical, slash, queries, keys_values.reshape(2, NC, CH, width))


def solution(mesh):
    NS, NH = mesh.shape["seq"], mesh.shape["head"]
    sizes = (NS, NH, NH // NX, NS // 2, 2 * NH, NS // 2)
    placed = (P(("seq", "head"), None), P(("seq", "head"), None), P(), P(), P())
    return jax.shard_map(
        functools.partial(on_device, sizes),
        mesh=mesh,
        in_specs=placed,
        out_specs=P(("seq", "head"), None, None),
        check_vma=False,
    )
```

time: 314 us -> 123 us (0.39)
  waiting for transfers between devices: 138 us -> 0 us
  Pallas kernels: 0 us -> 113 us
  matrix products: 68 us -> 0 us
  local copies, waits for them, and re-layouts: 44.4 us -> 9.03 us
  starting transfers between devices: 25.6 us -> 0 us
  other arithmetic: 18.4 us -> 0 us
  between operations: 14.1 us -> 0.02 us
  loops' own time: 3.51 us -> 0 us
    pallas_call x0 -> x2, Pallas kernels: none -> 113 us  [the longest x1 111 us: on_device(): pl.pallas_call(functools.partial(main_kernel, sizes), out_shape=jax.Shape...]
    all_to_all x2 -> x0, waiting for transfers between devices: 71.4 us -> none  [the longest x1 38.2 us: on_device(): lax.all_to_all(outgoing, 'head', split_axis=1, concat_axis=1, tiled=True)]
    dot_general x14 -> x0, matrix products: 68 us -> none  [the longest x4 24.2 us: vertical_step(): jnp.einsum('inqk,ikd->inqd', weights, values, preferred_element_type=jnp....]
    psum x1 -> x0, waiting for transfers between devices: 66.8 us -> none  [broadcast(): return lax.psum(block, axis)]
    gather x12 -> x0, local copies, waits for them, and re-layouts: 21.8 us -> none  [the longest x3 8.38 us: main_step(): fetched = key_store[local, :, store_heads[:, None]]]
    all_to_all x2 -> x0, starting transfers between devices: 20.5 us -> none  [the longest x1 13.7 us: on_device(): lax.all_to_all(shipped, 'head', split_axis=1, concat_axis=0, tiled=True)]
    reduce_sum x9 -> x0, other arithmetic: 8.7 us -> none  [the longest x7 8.47 us: softmax_update(): total = total * factor + jnp.sum(weights, axis=-1)]
    reshape x5 -> x1, local copies, waits for them, and re-layouts: 8.32 us -> 1.35 us  [on_device(): assignment.reshape(HQ, 1)]
  transfers between devices with their start and end apart: 4 -> 0, of which waited for: 3 -> 0; matrix products, arithmetic and copies ran while one was open for 21% -> 0% of each run, Pallas kernels for 0% -> 0%
where the time goes in v1:
time: 123 us; the launch traced here: 122 us
  Pallas kernels  113 us (92%)
  local copies, waits for them, and re-layouts  9.03 us (7%)
    pallas_call x1, Pallas kernels, on_device(): pl.pallas_call(functools.partial(main_kernel, sizes), out_shape=jax.Shape...  111 us
    unnamed x11, local copies, waits for them, and re-layouts  7.69 us

profile of v1, /device:TPU:1, one launch (start us, length us, event | category | flops | bytes accessed | tf_op | source)
XLA Modules:
  0.0 122.1 jit_solution(13479430903474527584)
XLA Ops:
  0.0 1.4 %copy.6.vert_ref = s32[64,4]{1,0:T(8,128)} copy(s32[64,4]{0,1:T(4,128)} %param.7) | data formatting | bytes 2048 | tf_op args[2]
  1.4 0.8 copy.9.slash_ref
  2.1 1.3 %copy.7.assign_ref = s32[64,1]{1,0:T(8,128)} copy(s32[64,1]{0,1:T(1,128)} %bitcast.3) | data formatting | bytes 512 | tf_op jit(solution)/shard_map/reshape | solution.py:338
  3.5 2.1 %shard_map.55.table = s32[128,128]{1,0:T(8,128)} custom-call(s32[64,4]{1,0:T(8,128)} %copy.6.vert_ref, s32[64,1]{1,0:T(8,128)} %copy.7.assign_ref), custom_call_target="tpu_custom_call" | custom-call | tf_op jit(solution)/shard_map/pallas_call | solution.py:333
  5.6 0.0 copy-start
  5.6 1.6 %copy-done = bf16[128,8192]{1,0:T(8,128)(2,1)S(1)} copy-done((bf16[128,8192]{1,0:T(8,128)(2,1)S(1)}, bf16[128,8192]{1,0:T(8,128)(2,1)}, u32[]{:S(2)}) %copy-start) | copy-done | bytes 2097176
  7.2 0.0 copy-start.1
  7.2 1.0 copy-done.1
  8.2 0.0 copy-start.2
  8.2 0.8 copy-done.2
  9.0 0.0 copy-start.3
  9.0 0.8 copy-done.3
  9.8 111.0 %shard_map.56 = bf16[2,4096,128]{2,1,0:T(8,128)(2,1)S(1)} custom-call(s32[128,128]{1,0:T(8,128)S(1)} %copy-done.3, s32[64,4]{1,0:T(8,128)S(1)} %copy-done.2, s32[64,2]{1,0:T(8,128)S(1)} %copy.9.slash_ref, bf16[128,8192]{1,0:T(8,128)(2,1)S(1)} %copy-done, bf16[2,4,16,2048]{3,2,1,0:T(8,128)(2,1)S(1)} %bitcast.2), custom_call_target="tpu_custom_call" | custom-call | tf_op jit(solution)/shard_map/pallas_call | solution.py:339
  120.8 1.3 %copy.11 = bf16[2,4096,128]{2,1,0:T(8,128)(2,1)} copy(bf16[2,4096,128]{2,1,0:T(8,128)(2,1)S(1)} %shard_map.56) | data formatting | bytes 4194304
Async XLA Ops:
  5.6 1.6 %copy-start = (bf16[128,8192]{1,0:T(8,128)(2,1)S(1)}, bf16[128,8192]{1,0:T(8,128)(2,1)}, u32[]{:S(2)}) copy-start(bf16[128,8192]{1,0:T(8,128)(2,1)} %q_hbm.1) | copy-start | bytes 6291460
  7.2 1.0 copy-start.1
  8.2 0.8 copy-start.2
  9.0 0.8 copy-start.3

commit v2 on v1

--- a/solution.py
+++ b/solution.py
@@ -20,8 +20,20 @@
 MESH = pl.DeviceIdType.MESH
 
 
-def table_kernel(group, vert_ref, assign_ref, out_ref):
-    v = vert_ref[...]
+def turned(rows):
+    m = rows.shape[1]
+    eye = (
+        lax.broadcasted_iota(jnp.int32, (m, m), 0) == lax.broadcasted_iota(jnp.int32, (m, m), 1)
+    ).astype(jnp.float32)
+    return lax.dot_general(
+        eye,
+        rows.astype(jnp.float32),
+        (((1,), (1,)), ((), ())),
+        preferred_element_type=jnp.float32,
+    ).astype(jnp.int32)
+
+
+def fill_table(group, v, assign, out_ref):
     heads = v.shape[0]
     block = lax.broadcasted_iota(jnp.int32, (heads, BLK), 1)
     used = jnp.zeros((heads, BLK), jnp.float32)
@@ -50,7 +62,7 @@
     head = lax.broadcasted_iota(jnp.int32, (heads, HD), 0)
     table = jnp.where(lane == 4, head.astype(jnp.float32), table)
     table = jnp.where(lane == 5, (head // group).astype(jnp.float32), table)
-    chosen = (assign_ref[...] % heads == other).astype(jnp.float32)
+    chosen = (assign % heads == other).astype(jnp.float32)
     out_ref[:heads] = table.astype(jnp.int32)
     slots = jnp.dot(chosen, table, preferred_element_type=jnp.float32)
     out_ref[heads:] = slots.astype(jnp.int32)
@@ -58,9 +70,9 @@
 
 def main_kernel(
     sizes,
-    table,
     vert_ref,
     slash_ref,
+    assign_ref,
     q_hbm,
     kv_hbm,
     out,
@@ -72,8 +84,10 @@
     stage,
     rows_bias,
     causal_bias,
+    table_v,
+    table,
     sems,
-    bar_free,
+    here_sem,
 ):
     NS, NH, NZ, NY, HQ, HK = sizes
     GQ = HQ // HK
@@ -95,20 +109,14 @@
 
     owner = b == home(a, x)
     source = seq == 0
+    last = (seq == NS - 1) & (head == NH - 1)
+    first = (seq == 0) & (head == 0)
     one = jnp.int32(1)
     nil = jnp.int32(0)
     own_source = jnp.where(owner & source, one, nil)
 
     def columns(n):
         return pl.ds(pl.multiple_of(n * HD, HD), HD)
-
-    @pl.loop(0, HQ)
-    def _(n):
-        pltpu.make_async_copy(q_hbm.at[:, columns(n)], q_v.at[n], sems.at[0]).start()
-
-    @pl.loop(0, 2 * HK)
-    def _(n):
-        pltpu.make_async_copy(kv_hbm.at[:, :, :, columns(n)], kcat.at[n, 1], sems.at[1]).start()
 
     barrier = pltpu.get_barrier_semaphore()
 
@@ -123,29 +131,37 @@
             def _():
                 greet(0, s)
 
-    @pl.loop(1, NH)
+    @pl.loop(1, NZ)
     def _(k):
-        greet(seq, (head + k) % NH)
+        greet(seq, (z + k) % NZ * NX + x)
 
     @pl.loop(1, NY)
     def _(k):
-        other = (y + k) % NY * 2 + core
-        greet(other, head)
-
-        @pl.when(core == 1)
-        def _():
-            for dx in range(1, NX):
-                greet(other, z * NX + (x + dx) % NX)
+        greet((y + k) % NY * 2 + core, head)
+
+    for k in range(1, NX):
+        greet(seq, z * NX + (x + k) % NX)
 
     greet(y * 2 + 1 - core, head)
 
-    @pl.when((head == 0) & (seq > 0))
-    def _():
-        greet(seq - 1, NH - 1)
+    @pl.when((x == 0) & jnp.logical_not(first))
+    def _():
+        greet(seq - jnp.where(head == 0, one, nil), (head + NH - 1) % NH)
+
+    @pl.loop(0, HQ)
+    def _(n):
+        pltpu.make_async_copy(q_hbm.at[:, columns(n)], q_v.at[n], sems.at[0]).start()
+
+    @pl.loop(0, 2 * HK)
+    def _(n):
+        pltpu.make_async_copy(kv_hbm.at[:, :, :, columns(n)], kcat.at[n, 1], sems.at[1]).start()
 
     base = (seq * NH + head) * 2
-    vert = vert_ref[...]
-    slash = slash_ref[...]
+    vert = turned(vert_ref[...])
+    slash = turned(slash_ref[...])
+    fill_table(GQ, vert, turned(assign_ref[...]), table_v)
+    to_smem = pltpu.make_async_copy(table_v, table, sems.at[14])
+    to_smem.start()
     lane = lax.broadcasted_iota(jnp.int32, (HQ, 8 * BLK), 1) // BLK
     target = base + lane - 2
     listed = jnp.full((HQ, 8 * BLK), -1, jnp.int32)
@@ -164,9 +180,10 @@
     col = lax.broadcasted_iota(jnp.int32, (ROWS, 2 * ROWS), 1) - ROWS
     causal_bias[...] = jnp.where(col <= row, 0.0, HIDE)
 
-    count = (NH - 1) + (NY - 1) * (1 + (NX - 1) * core) + 1
-    count = count + jnp.where((head == NH - 1) & (seq < NS - 1), one, nil)
+    count = (NZ - 1) + (NY - 1) + (NX - 1) + 1
+    count = count + jnp.where((x == NX - 1) & jnp.logical_not(last), one, nil)
     count = count + jnp.where(source, owners - own_source, nil)
+    to_smem.wait()
     pl.semaphore_wait(barrier, count)
 
     def remote(src, dst, send, recv, to):
@@ -179,6 +196,9 @@
             device_id_type=MESH,
         )
 
+    def entry(row, lane_, top):
+        return jnp.minimum(jnp.maximum(table[row, lane_], 0), top)
+
     def await_bytes(ref, sem):
         pltpu.make_async_copy(ref, ref, sems.at[sem]).wait()
 
@@ -200,8 +220,6 @@
             def _():
                 remote(src, dst, 2, 3, (s_, h_)).start()
 
-    last = (seq == NS - 1) & (head == NH - 1)
-    first = (seq == 0) & (head == 0)
     wrap = jnp.where(head == NH - 1, one, nil)
 
     @pl.when(jnp.logical_not(last))
@@ -215,11 +233,17 @@
     def _():
         kcat[:, 0] = jnp.zeros((2 * HK, *kcat.shape[2:]), kcat.dtype)
 
+    for k in range(1, NX):
+        pl.semaphore_signal(
+            here_sem, inc=1, device_id=(seq, z * NX + (x + k) % NX), device_id_type=MESH
+        )
+    pl.semaphore_wait(here_sem, NX - 1)
+
     @pl.when(owner)
     def _():
         await_bytes(tbuf, 3)
         for r in range(VPOOL):
-            piece[r] = tbuf[table[a * GQ, 8 + r]]
+            piece[r] = tbuf[entry(a * GQ, 8 + r, 2 * NH - 1)]
 
         @pl.loop(0, NZ * NX)
         def _(k):
@@ -256,41 +280,64 @@
     factor = math.log2(math.e) / math.sqrt(HD)
     contract = (((1,), (1,)), ((), ()))
 
-    def attend(slot):
-        h = table[HQ + slot, 4]
-        c = table[HQ + slot, 5]
-        query = q_v[h]
+    def attend(d):
+        c = entry(HQ + 2 * d, 5, HK - 1)
         keys = kcat[2 * c].reshape(2 * ROWS, HD)
         values = kcat[2 * c + 1].reshape(2 * ROWS, HD)
-        places = [table[HQ + slot, n] for n in range(NV)]
-        far_keys = jnp.concatenate([pool[0, c, p].reshape(BLK, HD) for p in places], axis=0)
-        far_values = jnp.concatenate([pool[1, c, p].reshape(BLK, HD) for p in places], axis=0)
-        bias = jnp.concatenate(
-            [jnp.broadcast_to(rows_bias[qb, h], (BLK, 8 * BLK)) for qb in range(2)],
-            axis=0,
+        heads = [entry(HQ + 2 * d + u, 4, HQ - 1) for u in range(2)]
+        queries = [q_v[h] for h in heads]
+        places = [
+            [entry(HQ + 2 * d + u, n, VPOOL - 1) for n in range(NV)] for u in range(2)
+        ]
+        seen = lax.dot_general(
+            jnp.concatenate(queries, axis=0), keys, contract, preferred_element_type=jnp.float32
         )
-        near = lax.dot_general(query, keys, contract, preferred_element_type=jnp.float32)
-        far = lax.dot_general(query, far_keys, contract, preferred_element_type=jnp.float32)
-        near = near * factor + (bias[:, : 2 * ROWS] + causal_bias[...])
-        far = far * factor + bias[:, 2 * ROWS :]
-        top = jnp.maximum(
-            jnp.max(near, axis=1, keepdims=True), jnp.max(far, axis=1, keepdims=True)
+        nears, totals, numers = [], [], []
+        for u in range(2):
+            far_keys = jnp.concatenate([pool[0, c, p].reshape(BLK, HD) for p in places[u]], axis=0)
+            far_values = jnp.concatenate(
+                [pool[1, c, p].reshape(BLK, HD) for p in places[u]], axis=0
+            )
+            far = lax.dot_general(
+                queries[u], far_keys, contract, preferred_element_type=jnp.float32
+            )
+            near = seen[u * ROWS : (u + 1) * ROWS] * factor + causal_bias[...]
+            near = jnp.concatenate(
+                [
+                    near[qb * BLK : (qb + 1) * BLK] + rows_bias[qb, heads[u]][:, : 2 * ROWS]
+                    for qb in range(2)
+                ],
+                axis=0,
+            )
+            far = far * factor
+            far = jnp.concatenate(
+                [
+                    far[qb * BLK : (qb + 1) * BLK] + rows_bias[qb, heads[u]][:, 2 * ROWS :]
+                    for qb in range(2)
+                ],
+                axis=0,
+            )
+            top = jnp.max(jnp.maximum(near, far), axis=1, keepdims=True)
+            near = jnp.exp2(near - top)
+            far = jnp.exp2(far - top)
+            totals.append(jnp.sum(near + far, axis=1, keepdims=True))
+            nears.append(near.astype(jnp.bfloat16))
+            numers.append(
+                jnp.dot(far.astype(jnp.bfloat16), far_values, preferred_element_type=jnp.float32)
+            )
+        joint = jnp.dot(
+            jnp.concatenate(nears, axis=0), values, preferred_element_type=jnp.float32
         )
-        near = jnp.exp2(near - top)
-        far = jnp.exp2(far - top)
-        total = jnp.sum(near, axis=1, keepdims=True) + jnp.sum(far, axis=1, keepdims=True)
-        numer = jnp.dot(
-            near.astype(jnp.bfloat16), values, preferred_element_type=jnp.float32
-        ) + jnp.dot(far.astype(jnp.bfloat16), far_values, preferred_element_type=jnp.float32)
-        stage[slot] = (numer / total).astype(jnp.bfloat16)
+        for u in range(2):
+            numer = joint[u * ROWS : (u + 1) * ROWS] + numers[u]
+            stage[2 * d + u] = (numer / totals[u]).astype(jnp.bfloat16)
 
     here = pl.ds(pl.multiple_of(head * ROWS, ROWS), ROWS)
 
     @pl.loop(1, NH + 1)
     def _(k):
         d = (head + k) % NH
-        attend(2 * d)
-        attend(2 * d + 1)
+        attend(d)
         src = stage.at[pl.ds(2 * d, 2)]
         dst = out.at[:, here]
 
@@ -328,18 +375,11 @@
     NS, NH, NZ, NY, HQ, HK = sizes
     width = keys_values.shape[1]
     vmem = pl.BlockSpec(memory_space=pltpu.VMEM)
-    smem = pl.BlockSpec(memory_space=pltpu.SMEM)
     hbm = pl.BlockSpec(memory_space=pl.ANY)
-    table = pl.pallas_call(
-        functools.partial(table_kernel, HQ // HK),
-        out_shape=jax.ShapeDtypeStruct((2 * HQ, HD), jnp.int32),
-        in_specs=[vmem, vmem],
-        out_specs=vmem,
-    )(vertical, assignment.reshape(HQ, 1))
     return pl.pallas_call(
         functools.partial(main_kernel, sizes),
         out_shape=jax.ShapeDtypeStruct((2, NH * ROWS, HD), jnp.bfloat16),
-        in_specs=[smem, vmem, vmem, hbm, hbm],
+        in_specs=[vmem, vmem, vmem, hbm, hbm],
         out_specs=hbm,
         scratch_shapes=[
             pltpu.VMEM((HQ, ROWS, HD), jnp.bfloat16),
@@ -350,13 +390,21 @@
             pltpu.VMEM((max(2 * NH, 2 * HK * NC), ROWS, HD), jnp.bfloat16),
             pltpu.VMEM((2, HQ, 1, 8 * BLK), jnp.float32),
             pltpu.VMEM((ROWS, 2 * ROWS), jnp.float32),
-            pltpu.SemaphoreType.DMA((14,)),
+            pltpu.VMEM((2 * HQ, HD), jnp.int32),
+            pltpu.SMEM((2 * HQ, HD), jnp.int32),
+            pltpu.SemaphoreType.DMA((15,)),
             pltpu.SemaphoreType.REGULAR,
         ],
         compiler_params=pltpu.CompilerParams(
-            collective_id=0, has_side_effects=True, vmem_limit_bytes=40 * 2**20
+            collective_id=0, has_side_effects=True, vmem_limit_bytes=60 * 2**20
         ),
-    )(table, vertical, slash, queries, keys_values.reshape(2, NC, CH, width))
+    )(
+        vertical.T,
+        slash.T,
+        assignment.reshape(1, HQ),
+        queries,
+        keys_values.reshape(2, NC, CH, width),
+    )
 
 
 def solution(mesh):

time: 123 us -> 110 us (0.89)
  Pallas kernels: 113 us -> 107 us
  local copies, waits for them, and re-layouts: 9.03 us -> 3.05 us
    unnamed x11 -> x1, local copies, waits for them, and re-layouts: 7.69 us -> 3.05 us
    pallas_call x1, Pallas kernels: 111 us -> 107 us  [on_device(): pl.pallas_call(functools.partial(main_kernel, sizes), out_shape=jax.Shape...]
    pallas_call x1 -> x0, Pallas kernels: 2.08 us -> none  [on_device(): pl.pallas_call(functools.partial(table_kernel, HQ // HK), out_shape=jax.S...]
    reshape x1 -> x0, local copies, waits for them, and re-layouts: 1.35 us -> none  [on_device(): assignment.reshape(HQ, 1)]
where the time goes in v2:
time: 110 us
  Pallas kernels  107 us (97%)
  local copies, waits for them, and re-layouts  3.05 us (3%)
    pallas_call x1, Pallas kernels, on_device(): pl.pallas_call(functools.partial(main_kernel, sizes), out_shape=jax.Shape...  107 us
    unnamed x1, local copies, waits for them, and re-layouts  3.05 us

profile of v2, /device:TPU:1, one launch (start us, length us, event | category | flops | bytes accessed | tf_op | source)
XLA Modules:
  0.0 109.6 jit_solution(1110821887437035207)
XLA Ops:
  0.0 106.5 %shard_map.55 = bf16[2,4096,128]{2,1,0:T(8,128)(2,1)} custom-call(s32[4,64]{1,0:T(4,128)} %bitcast.5, s32[2,64]{1,0:T(2,128)} %bitcast.6, s32[1,64]{1,0:T(1,128)} %bitcast.7, bf16[128,8192]{1,0:T(8,128)(2,1)} %q_hbm.1, bf16[2,4,16,2048]{3,2,1,0:T(8,128)(2,1)} %bitcast.4), custom_call_target="tpu_custom_call" | custom-call | tf_op jit(solution)/shard_map/pallas_call | solution.py:379
  106.5 3.0 %copy.7 = bf16[2,4096,128]{2,1,0:T(8,128)(2,1)} copy(bf16[2,4096,128]{2,1,0:T(8,128)(2,1)} %shard_map.55) | data formatting | bytes 4194304

commit v3 on v2

--- a/solution.py
+++ b/solution.py
@@ -199,6 +199,9 @@
     def entry(row, lane_, top):
         return jnp.minimum(jnp.maximum(table[row, lane_], 0), top)
 
+    def far_first(place, k, size):
+        return (place + size // 2 + (k + 1) // 2 * (1 - 2 * (k % 2)) + size) % size
+
     def await_bytes(ref, sem):
         pltpu.make_async_copy(ref, ref, sems.at[sem]).wait()
 
@@ -261,9 +264,10 @@
 
     await_bytes(pool.at[core, a], 7)
 
-    @pl.loop(1, NY)
+    @pl.loop(0, NY - 1)
     def _(k):
-        remote(pool.at[core, a], pool.at[core, a], 8, 9, device(core, (a + k) % NY, b, x)).start()
+        to = device(core, far_first(a, k, NY), b, x)
+        remote(pool.at[core, a], pool.at[core, a], 8, 9, to).start()
 
     await_bytes(pool.at[core, pl.ds(0, NY - 1)], 9)
     swap = remote(pool.at[core], pool.at[core], 10, 11, (y * 2 + 1 - core, head))
@@ -334,18 +338,18 @@
 
     here = pl.ds(pl.multiple_of(head * ROWS, ROWS), ROWS)
 
-    @pl.loop(1, NH + 1)
+    @pl.loop(0, NH)
     def _(k):
-        d = (head + k) % NH
+        d = far_first(z, k // NX, NZ) * NX + (x + 1 + k) % NX
         attend(d)
         src = stage.at[pl.ds(2 * d, 2)]
         dst = out.at[:, here]
 
-        @pl.when(k == NH)
+        @pl.when(k == NH - 1)
         def _():
             pltpu.make_async_copy(src, dst, sems.at[13]).start()
 
-        @pl.when(k < NH)
+        @pl.when(k < NH - 1)
         def _():
             remote(src, dst, 12, 13, (seq, d)).start()
 

time: 110 us -> 103 us (0.936)
  Pallas kernels: 107 us -> 99.8 us
    pallas_call x1, Pallas kernels: 107 us -> 99.8 us  [on_device(): pl.pallas_call(functools.partial(main_kernel, sizes), out_shape=jax.Shape...]
where the time goes in v3:
time: 103 us
  Pallas kernels  99.8 us (97%)
  local copies, waits for them, and re-layouts  3.05 us (3%)
    pallas_call x1, Pallas kernels, on_device(): pl.pallas_call(functools.partial(main_kernel, sizes), out_shape=jax.Shape...  99.8 us
    unnamed x1, local copies, waits for them, and re-layouts  3.05 us

profile of v3, /device:TPU:1, one launch (start us, length us, event | category | flops | bytes accessed | tf_op | source)
XLA Modules:
  0.0 102.9 jit_solution(5096783801187823654)
XLA Ops:
  0.0 99.8 %shard_map.55 = bf16[2,4096,128]{2,1,0:T(8,128)(2,1)} custom-call(s32[4,64]{1,0:T(4,128)} %bitcast.5, s32[2,64]{1,0:T(2,128)} %bitcast.6, s32[1,64]{1,0:T(1,128)} %bitcast.7, bf16[128,8192]{1,0:T(8,128)(2,1)} %q_hbm.1, bf16[2,4,16,2048]{3,2,1,0:T(8,128)(2,1)} %bitcast.4), custom_call_target="tpu_custom_call" | custom-call | tf_op jit(solution)/shard_map/pallas_call | solution.py:383
  99.8 3.0 %copy.7 = bf16[2,4096,128]{2,1,0:T(8,128)(2,1)} copy(bf16[2,4096,128]{2,1,0:T(8,128)(2,1)} %shard_map.55) | data formatting | bytes 4194304

commit v4 on v3

--- a/solution.py
+++ b/solution.py
@@ -123,6 +123,23 @@
     def greet(s_, h_):
         pl.semaphore_signal(barrier, inc=1, device_id=(s_, h_), device_id_type=MESH)
 
+    @pl.loop(1, NZ)
+    def _(k):
+        greet(seq, (z + k) % NZ * NX + x)
+
+    @pl.loop(1, NY)
+    def _(k):
+        greet((y + k) % NY * 2 + core, head)
+
+    for k in range(1, NX):
+        greet(seq, z * NX + (x + k) % NX)
+
+    greet(y * 2 + 1 - core, head)
+
+    @pl.when((x == 0) & jnp.logical_not(first))
+    def _():
+        greet(seq - jnp.where(head == 0, one, nil), (head + NH - 1) % NH)
+
     @pl.when(owner)
     def _():
         @pl.loop(0, NH)
@@ -130,23 +147,6 @@
             @pl.when(jnp.logical_not(source & (head == s)))
             def _():
                 greet(0, s)
-
-    @pl.loop(1, NZ)
-    def _(k):
-        greet(seq, (z + k) % NZ * NX + x)
-
-    @pl.loop(1, NY)
-    def _(k):
-        greet((y + k) % NY * 2 + core, head)
-
-    for k in range(1, NX):
-        greet(seq, z * NX + (x + k) % NX)
-
-    greet(y * 2 + 1 - core, head)
-
-    @pl.when((x == 0) & jnp.logical_not(first))
-    def _():
-        greet(seq - jnp.where(head == 0, one, nil), (head + NH - 1) % NH)
 
     @pl.loop(0, HQ)
     def _(n):
@@ -209,7 +209,7 @@
     def _():
         @pl.loop(0, owners)
         def _(o):
-            core_, a_, c_ = o // (HK * NC), o // NC % HK, o % NC
+            core_, a_, c_ = o // (HK * NC), o % HK, o // HK % NC
             s_, h_ = device(core_, a_, home(a_, c_), c_)
             src = kv_hbm.at[:, c_, :, columns(2 * a_ + core_)]
             dst = tbuf.at[pl.ds(2 * head, 2)]
@@ -224,13 +224,6 @@
                 remote(src, dst, 2, 3, (s_, h_)).start()
 
     wrap = jnp.where(head == NH - 1, one, nil)
-
-    @pl.when(jnp.logical_not(last))
-    def _():
-        @pl.loop(0, 2 * HK)
-        def _(n):
-            src = kv_hbm.at[:, :, :, columns(n)]
-            remote(src, kcat.at[n, 0], 4, 5, (seq + wrap, (head + 1) % NH)).start()
 
     @pl.when(first)
     def _():
@@ -262,16 +255,30 @@
             def _():
                 remote(piece, dst, 6, 7, device(core, a, b_, x_)).start()
 
+    @pl.when(jnp.logical_not(last))
+    def _():
+        @pl.loop(0, 2 * HK)
+        def _(n):
+            src = kv_hbm.at[:, :, :, columns(n)]
+            remote(src, kcat.at[n, 0], 4, 5, (seq + wrap, (head + 1) % NH)).start()
+
     await_bytes(pool.at[core, a], 7)
 
     @pl.loop(0, NY - 1)
     def _(k):
         to = device(core, far_first(a, k, NY), b, x)
-        remote(pool.at[core, a], pool.at[core, a], 8, 9, to).start()
-
-    await_bytes(pool.at[core, pl.ds(0, NY - 1)], 9)
-    swap = remote(pool.at[core], pool.at[core], 10, 11, (y * 2 + 1 - core, head))
-    swap.start()
+        remote(pool.at[core, a], pool.at[core, a], 8, 15 + a, to).start()
+
+    @pl.loop(0, HK)
+    def _(k):
+        a_ = far_first(a, HK - 1 - k, HK)
+
+        @pl.when(k > 0)
+        def _():
+            await_bytes(pool.at[core, a_], 15 + a_)
+
+        remote(pool.at[core, a_], pool.at[core, a_], 10, 11, (y * 2 + 1 - core, head)).start()
+
     await_bytes(q_v, 0)
     await_bytes(kcat.at[:, 1], 1)
 
@@ -396,7 +403,7 @@
             pltpu.VMEM((ROWS, 2 * ROWS), jnp.float32),
             pltpu.VMEM((2 * HQ, HD), jnp.int32),
             pltpu.SMEM((2 * HQ, HD), jnp.int32),
-            pltpu.SemaphoreType.DMA((15,)),
+            pltpu.SemaphoreType.DMA((15 + HK,)),
             pltpu.SemaphoreType.REGULAR,
         ],
         compiler_params=pltpu.CompilerParams(

time: 103 us -> 103 us (level)
  no operation moved by 1% of the time
where the time goes in v4:
time: 103 us
  Pallas kernels  99.5 us (97%)
  local copies, waits for them, and re-layouts  3.05 us (3%)
    pallas_call x1, Pallas kernels, on_device(): pl.pallas_call(functools.partial(main_kernel, sizes), out_shape=jax.Shape...  99.5 us
    unnamed x1, local copies, waits for them, and re-layouts  3.05 us

profile of v4, /device:TPU:1, one launch (start us, length us, event | category | flops | bytes accessed | tf_op | source)
XLA Modules:
  0.0 102.6 jit_solution(10355874728019977781)
XLA Ops:
  0.0 99.5 %shard_map.55 = bf16[2,4096,128]{2,1,0:T(8,128)(2,1)} custom-call(s32[4,64]{1,0:T(4,128)} %bitcast.5, s32[2,64]{1,0:T(2,128)} %bitcast.6, s32[1,64]{1,0:T(1,128)} %bitcast.7, bf16[128,8192]{1,0:T(8,128)(2,1)} %q_hbm.1, bf16[2,4,16,2048]{3,2,1,0:T(8,128)(2,1)} %bitcast.4), custom_call_target="tpu_custom_call" | custom-call | tf_op jit(solution)/shard_map/pallas_call | solution.py:390
  99.5 3.0 %copy.7 = bf16[2,4096,128]{2,1,0:T(8,128)(2,1)} copy(bf16[2,4096,128]{2,1,0:T(8,128)(2,1)} %shard_map.55) | data formatting | bytes 4194304
